TPU v7x, 32 devices: a whole 2x2x4 slice. The times are simulated.
32 devices in a mesh: tmpl: 16 (over z, y, x), sta: 2 (over core).
Axes of the slice: x: 2, y: 2, z: 4, core: 2. Of those that a mesh axis runs over, the one named last changes fastest.
Arguments:
- records: float32 [152, 2048], P('sta', 'tmpl'), may hold values from -6 to 6
- templates: float32 [64, 152, 600], P('tmpl', 'sta'), may hold values from -6 to 6
- offsets: int32 [64, 152], P('tmpl', 'sta'), may hold values from 0 to 425
- available: int32 [64, 152], P('tmpl', 'sta'), may hold values 0 or 1
Outputs:
- detection: float32 [64, 1024], P('tmpl', 'sta')
All inputs are finite; a program needn't handle non-finite values. No bound on the sum of `available` on one device may be relied on, other than what follows from the above.
Results may differ from a plain program's by a relative error of at most 0.0066.
Values may be sent and summed in bfloat16 or wider, within the bound.
A program may use at most 64 MiB of HBM per device.

v0:
```python
import functools

import jax
import jax.numpy as jnp
from jax import lax
from jax.experimental import pallas as pl
from jax.experimental.pallas import tpu as pltpu
from jax.sharding import PartitionSpec as P

OFFMAX = 425
LANES = 128
STEP = 32
PARTS = LANES // STEP


def round_up(value, unit):
    return (value + unit - 1) // unit * unit


def largest_divisor(value, most):
    return max(d for d in range(1, most + 1) if value % d == 0)


def split_three(values):
    high = values.astype(jnp.bfloat16)
    rest = values - high.astype(jnp.float32)
    middle = rest.astype(jnp.bfloat16)
    low = (rest - middle.astype(jnp.float32)).astype(jnp.bfloat16)
    return jnp.concatenate([high, middle, low], axis=1)


def correlate_kernel(
    sizes, offsets_ref, available_ref, records_ref, templates_ref, out_ref,
    centred_ref, inverse_ref, rows_ref, sums_ref, scale_ref, shifted_ref, copies_ref, picks_ref,
):
    templ_here, channels, length, blocks, lag_rows, pos_rows, pad_rows, width, group = sizes
    whole, part = length // LANES, length % LANES
    lane = lax.broadcasted_iota(jnp.int32, (1, LANES), 1)

    centred_ref[...] = jnp.zeros_like(centred_ref)
    for t in range(templ_here):
        shapes = templates_ref[t]
        centred = shapes - jnp.sum(shapes, axis=1, keepdims=True) / length
        power = jnp.sum(centred * centred, axis=1, keepdims=True)
        centred_ref[t, :, :length] = centred
        inverse_ref[t] = jnp.broadcast_to(1.0 / jnp.sqrt(power + 1e-05), (channels, LANES))

    row = lax.broadcasted_iota(jnp.int32, (LANES, 2 * LANES), 0)
    column = lax.broadcasted_iota(jnp.int32, (LANES, 2 * LANES), 1)
    ones = jnp.where((row < column) | (column >= LANES), 1.0, 0.0).astype(jnp.bfloat16)
    ones = jnp.concatenate([ones, ones, ones], axis=0)
    rows_ref[...] = jnp.zeros_like(rows_ref)
    sums_ref[...] = jnp.zeros_like(sums_ref)

    def scale_group(g, carry):
        block = records_ref[pl.ds(g * group, group)].reshape(group * blocks, LANES)
        both = jnp.concatenate([split_three(block), split_three(block * block)], axis=0)
        sums = jnp.dot(both, ones, preferred_element_type=jnp.float32)
        for i in range(group):
            windows = []
            for kind in range(2):
                at = (kind * group + i) * blocks
                slot = i * 2 + kind
                sums_ref[slot, :blocks, :] = sums[at : at + blocks]
                inside = lambda first: sums_ref[slot, first : first + pos_rows, :LANES]
                total = lambda first: sums_ref[slot, first : first + pos_rows, LANES:]
                near, far = inside(whole), inside(whole + 1)
                if part:
                    near = pltpu.roll(near, LANES - part, 1)
                    far = pltpu.roll(far, LANES - part, 1)
                window = jnp.where(lane < LANES - part, near, far + total(whole)) - inside(0)
                for b in range(whole):
                    window = window + total(b)
                windows.append(window)
            energy = windows[1] - windows[0] * windows[0] / length
            scale_ref[g * group + i] = 1.0 / jnp.sqrt(energy + 1e-05)
        return carry

    lax.fori_loop(0, channels // group, scale_group, 0)

    def channel(c, slot, totals):
        rows_ref[slot, :blocks, :] = records_ref[c]
        reach = pad_rows - 8
        here = rows_ref[slot, :reach, :]
        after = rows_ref[slot, 1 : reach + 1, :]
        for u in range(PARTS):
            if u == 0:
                moved = here
            else:
                moved = jnp.where(
                    lane < LANES - STEP * u,
                    pltpu.roll(here, LANES - STEP * u, 1),
                    pltpu.roll(after, LANES - STEP * u, 1),
                )
            shifted_ref[slot, u, :reach, :] = moved
        frames = jnp.concatenate(
            [
                jnp.concatenate(
                    [
                        shifted_ref[slot, u, j : j + pos_rows, :].astype(jnp.bfloat16)
                        for j in range(width // LANES)
                    ],
                    axis=1,
                )
                for u in range(PARTS)
            ],
            axis=0,
        )
        for t in range(templ_here):
            wave = jnp.broadcast_to(centred_ref[t, pl.ds(c, 1), :], (8, width))
            first = pltpu.roll(wave, 0, 1, stride=1, stride_axis=0)
            for h in range(STEP // 16):
                pair = [
                    first if s == 0 else pltpu.roll(first, s, 1) for s in (16 * h, 16 * h + 8)
                ]
                copies_ref[slot, pl.ds(t * STEP + 16 * h, 16), :] = jnp.concatenate(
                    pair, axis=0
                ).astype(jnp.bfloat16)
        product = lax.dot_general(
            frames, copies_ref[slot], (((1,), (1,)), ((), ())), preferred_element_type=jnp.float32
        )
        scale = scale_ref[c]
        turned = {}
        for u in range(PARTS):
            piece = product[u * pos_rows : (u + 1) * pos_rows]
            for k in range(PARTS):
                turned[u, k] = piece if k == 0 else pltpu.roll(piece, STEP * k, 1)
        result = []
        for t in range(templ_here):
            values = turned[0, (-t) % PARTS]
            for u in range(1, PARTS):
                values = jnp.where(lane >= STEP * u, turned[u, (u - t) % PARTS], values)
            picks_ref[slot, t] = values * scale
            offset = offsets_ref[t, c]
            down, right = offset // LANES, offset % LANES
            near = picks_ref[slot, t, pl.ds(down, lag_rows), :]
            far = picks_ref[slot, t, pl.ds(down + 1, lag_rows), :]
            picked = jnp.where(lane >= right, near, far)
            weight = inverse_ref[t, pl.ds(c, 1), :] * available_ref[t, c].astype(jnp.float32)
            picked = pltpu.roll(picked * weight, (LANES - right) % LANES, 1)
            result.append(totals[t] + picked)
        return tuple(result)

    def channel_group(g, totals):
        for i in range(group):
            totals = channel(g * group + i, i, totals)
        return totals

    empty = tuple(jnp.zeros((lag_rows, LANES), jnp.float32) for _ in range(templ_here))
    totals = lax.fori_loop(0, channels // group, channel_group, empty)
    for t in range(templ_here):
        out_ref[t] = totals[t]


def correlate(records, templates, offsets, available):
    channels, blocks, _ = records.shape
    templ_here, _, length = templates.shape
    lag_count = blocks * LANES - OFFMAX - length + 1
    lag_rows = lag_count // LANES
    pos_rows = round_up(lag_rows + (OFFMAX + LANES - 1) // LANES, 16)
    width = round_up(length + STEP - 1, LANES)
    pad_rows = round_up(max(pos_rows + width // LANES, blocks) + 1, 8) + 8
    group = largest_divisor(channels, 4)
    sizes = (templ_here, channels, length, blocks, lag_rows, pos_rows, pad_rows, width, group)
    macs = channels * templ_here * STEP * width * PARTS * pos_rows
    return pl.pallas_call(
        functools.partial(correlate_kernel, sizes),
        out_shape=jax.ShapeDtypeStruct((templ_here, lag_rows, LANES), jnp.float32),
        in_specs=[pl.BlockSpec(memory_space=pltpu.SMEM)] * 2
        + [pl.BlockSpec(memory_space=pltpu.VMEM)] * 2,
        out_specs=pl.BlockSpec(memory_space=pltpu.VMEM),
        scratch_shapes=[
            pltpu.VMEM((templ_here, channels, width), jnp.float32),
            pltpu.VMEM((templ_here, channels, LANES), jnp.float32),
            pltpu.VMEM((group, pad_rows, LANES), jnp.float32),
            pltpu.VMEM((2 * group, pad_rows, 2 * LANES), jnp.float32),
            pltpu.VMEM((channels, pos_rows, LANES), jnp.float32),
            pltpu.VMEM((group, PARTS, pad_rows, LANES), jnp.float32),
            pltpu.VMEM((group, templ_here * STEP, width), jnp.bfloat16),
            pltpu.VMEM((group, templ_here, pos_rows, LANES), jnp.float32),
        ],
        compiler_params=pltpu.CompilerParams(vmem_limit_bytes=32 * 1024 * 1024),
        cost_estimate=pl.CostEstimate(
            flops=2 * macs, bytes_accessed=4 * (records.size + templates.size), transcendentals=0
        ),
    )(offsets, available, records, templates)


def shards(records, templates, offsets, available):
    channels_here = records.shape[0]
    whole = lax.all_gather(records, "tmpl", axis=1, tiled=True)
    whole = whole.reshape(channels_here, whole.shape[1] // LANES, LANES)
    partial = correlate(whole, templates, offsets, available)
    partial_stack = partial.reshape(partial.shape[0], -1)
    lag_count = partial_stack.shape[1]
    share = lag_count // lax.axis_size("sta")
    full_stack = lax.psum(partial_stack, "sta")
    power = jnp.mean(full_stack * full_stack, axis=1, keepdims=True)
    mine = lax.dynamic_slice_in_dim(full_stack, lax.axis_index("sta") * share, share, 1)
    return mine / jnp.sqrt(power + 1e-05)


def solution(mesh):
    in_specs = (P("sta", "tmpl"), P("tmpl", "sta", None), P("tmpl", "sta"), P("tmpl", "sta"))
    out_specs = P("tmpl", "sta")
    return jax.shard_map(shards, mesh=mesh, in_specs=in_specs, out_specs=out_specs, check_vma=False)
```

profile of v0, /device:TPU:0, one launch (start us, length us, event | category | flops | bytes accessed | tf_op | source)
XLA Modules:
  0.0 75.5 jit_solution(12228286707390770597)
XLA Ops:
  0.0 46.5 %all_gather.3 = f32[76,2048]{1,0:T(8,128)S(1)} all-gather(f32[76,128]{1,0:T(8,128)} %param.4), channel_id=1, replica_groups=mesh['tmpl'=16,'sta'=2] {'tmpl'}, dimensions={1}, use_global_device_ids=true | all-gather | bytes 661504 | tf_op jit(solution)/shard_map/all_gather | solution.py:191
  46.5 0.1 copy.6
  46.6 0.0 copy-start.2
  46.7 1.1 %copy-done.2 = f32[4,76,600]{2,0,1:T(4,128)S(1)} copy-done((f32[4,76,600]{2,0,1:T(4,128)S(1)}, f32[4,76,600]{2,0,1:T(4,128)}, u32[]{:S(2)}) %copy-start.2) | copy-done | bytes 729624
  47.7 0.0 copy-start
  47.7 0.0 copy-start.1
  47.8 0.1 copy.5.templates_ref
  47.8 0.6 copy-done
  48.4 0.0 copy-done.1
  48.4 22.8 %shard_map.46 = f32[4,8,128]{2,1,0:T(8,128)S(1)} custom-call(s32[4,76]{1,0:T(4,128)S(1)} %copy-done, s32[4,76]{1,0:T(4,128)S(1)} %copy-done.1, f32[76,16,128]{2,1,0:T(8,128)S(1)} %slice.records_ref, f32[4,76,600]{2,1,0:T(8,128)S(1)} %copy.5.templates_ref), custom_call_target="tpu_custom_call" | custom-call | flops 796917760 | bytes 1352192 | tf_op jit(solution)/shard_map/pallas_call | solution.py:166
  71.3 3.4 %psum.7 = f32[4,1024]{1,0:T(4,128)S(1)} all-reduce(f32[4,1024]{1,0:T(4,128)S(1)} %bitcast.10), channel_id=1, replica_groups=mesh['tmpl'=16,'sta'=2] {'sta'}, use_global_device_ids=true, to_apply=%region_0.0 | all-reduce | flops 4096 | bytes 32768 | tf_op jit(solution)/shard_map/psum | solution.py:197
  74.6 0.1 multiply_reduce_fusion
  74.8 0.7 dynamic-slice_divide_fusion
  (3 shorter events, 0.1 us)
Async XLA Ops:
  46.6 1.1 %copy-start.2 = (f32[4,76,600]{2,0,1:T(4,128)S(1)}, f32[4,76,600]{2,0,1:T(4,128)}, u32[]{:S(2)}) copy-start(f32[4,76,600]{2,0,1:T(4,128)} %param.5) | copy-start | bytes 2188804
  47.7 0.7 copy-start
  47.7 0.7 copy-start.1
where the time goes:
time: 75.7 us; the launch traced here: 75.5 us
  blocking collectives  49.8 us (66%)
  Pallas kernels  22.8 us (30%)
  local copies, waits for them, and re-layouts  1.93 us (3%)
  other arithmetic  0.82 us (1%)
    all_gather x1, blocking collectives, shards(): whole = lax.all_gather(records, 'tmpl', axis=1, tiled=True)  46.5 us
    pallas_call x1, Pallas kernels, correlate(): pl.pallas_call(functools.partial(correlate_kernel, sizes), out_shape=jax....  22.8 us
    psum x1, blocking collectives, shards(): full_stack = lax.psum(partial_stack, 'sta')  3.36 us
    unnamed x9, local copies, waits for them, and re-layouts  1.89 us

commit v1 on v0

v1 whole, which is shorter than its diff:
```python
import functools

import jax
import jax.numpy as jnp
from jax import lax
from jax.experimental import pallas as pl
from jax.experimental.pallas import tpu as pltpu
from jax.sharding import PartitionSpec as P

OFFMAX = 425
LANES = 128
STEP = 32
PARTS = LANES // STEP


def round_up(value, unit):
    return (value + unit - 1) // unit * unit


def largest_divisor(value, most):
    return max(d for d in range(1, most + 1) if value % d == 0)


def split_three(values):
    high = values.astype(jnp.bfloat16)
    rest = values - high.astype(jnp.float32)
    middle = rest.astype(jnp.bfloat16)
    low = (rest - middle.astype(jnp.float32)).astype(jnp.bfloat16)
    return jnp.concatenate([high, middle, low], axis=1)


def detect_kernel(
    sizes, offsets_ref, available_ref, records_ref, templates_ref, out_ref,
    gathered_ref, series_ref, centred_ref, inverse_ref, sums_ref, scale_ref, shifted_ref,
    copies_ref, picks_ref, stacks_ref, send_near, recv_near, send_far, recv_far, send_stack, recv_stack,
):
    (templ_here, channels, length, outer, inner, stations, lag_rows, pos_rows, pad_rows, width,
     group, slot_rows) = sizes
    blocks = outer * inner
    whole, part = length // LANES, length % LANES
    lane = lax.broadcasted_iota(jnp.int32, (1, LANES), 1)
    place, station = lax.axis_index("tmpl"), lax.axis_index("sta")
    mine_out, mine_in = place // inner, place % inner

    def far_peer(k):
        return (lax.rem(mine_out + k, outer) * inner + mine_in, station)

    def near_peer(k):
        return (mine_out * inner + lax.rem(mine_in + k, inner), station)

    def stack_peer(k):
        return (place, lax.rem(station + k, stations))

    peers = [far_peer(k) for k in range(1, outer)]
    peers += [near_peer(k) for k in range(1, inner)]
    peers += [stack_peer(k) for k in range(1, stations)]
    barrier = pltpu.get_barrier_semaphore()
    for peer in peers:
        pl.semaphore_signal(barrier, inc=1, device_id=peer, device_id_type=pl.DeviceIdType.MESH)

    own = pl.ds(pl.multiple_of((mine_in * outer + mine_out) * slot_rows, 8), slot_rows)
    if slot_rows > channels:
        tail = jnp.zeros((slot_rows - channels, LANES), jnp.float32)
        gathered_ref[own, :] = jnp.concatenate([records_ref[...], tail], axis=0)
    else:
        gathered_ref[own, :] = records_ref[...]
    pl.semaphore_wait(barrier, len(peers))

    def send(part_ref, send_sem, recv_sem, peer):
        copy = pltpu.make_async_remote_copy(
            src_ref=part_ref, dst_ref=part_ref, send_sem=send_sem, recv_sem=recv_sem,
            device_id=peer, device_id_type=pl.DeviceIdType.MESH,
        )
        copy.start()
        return copy

    far_copies = [
        send(gathered_ref.at[own], send_far.at[k], recv_far.at[k], far_peer(k))
        for k in range(1, outer)
    ]

    centred_ref[...] = jnp.zeros_like(centred_ref)
    for t in range(templ_here):
        shapes = templates_ref[t]
        centred = shapes - jnp.sum(shapes, axis=1, keepdims=True) / length
        power = jnp.sum(centred * centred, axis=1, keepdims=True)
        centred_ref[t, :, :length] = centred
        inverse_ref[t] = jnp.broadcast_to(1.0 / jnp.sqrt(power + 1e-05), (channels, LANES))
    series_ref[...] = jnp.zeros_like(series_ref)
    sums_ref[...] = jnp.zeros_like(sums_ref)

    def delay_group(g, carry):
        for i in range(group):
            c = g * group + i
            for t in range(templ_here):
                wave = jnp.broadcast_to(centred_ref[t, pl.ds(c, 1), :], (8, width))
                first = pltpu.roll(wave, 0, 1, stride=1, stride_axis=0)
                for h in range(STEP // 16):
                    pair = [
                        first if s == 0 else pltpu.roll(first, s, 1)
                        for s in (16 * h, 16 * h + 8)
                    ]
                    copies_ref[c, t * STEP + 16 * h : t * STEP + 16 * h + 16, :] = (
                        jnp.concatenate(pair, axis=0).astype(jnp.bfloat16)
                    )
        return carry

    groups = channels // group
    early = groups // 3
    lax.fori_loop(0, early, delay_group, 0)
    for copy in far_copies:
        copy.wait_recv()
    lane_rows = pl.ds(pl.multiple_of(mine_in * outer * slot_rows, 8), outer * slot_rows)
    near_copies = [
        send(gathered_ref.at[lane_rows], send_near.at[k], recv_near.at[k], near_peer(k))
        for k in range(1, inner)
    ]
    lax.fori_loop(early, groups, delay_group, 0)
    for copy in near_copies:
        copy.wait_recv()
    for copy in far_copies + near_copies:
        copy.wait_send()

    row = lax.broadcasted_iota(jnp.int32, (LANES, 2 * LANES), 0)
    column = lax.broadcasted_iota(jnp.int32, (LANES, 2 * LANES), 1)
    ones = jnp.where((row < column) | (column >= LANES), 1.0, 0.0).astype(jnp.bfloat16)
    ones = jnp.concatenate([ones, ones, ones], axis=0)

    def scale_group(g, carry):
        for i in range(group):
            c = g * group + i
            for o in range(outer):
                series_ref[c, o * inner : (o + 1) * inner, :] = gathered_ref[
                    pl.ds(o * slot_rows + c, inner, stride=outer * slot_rows), :
                ]
        block = jnp.concatenate(
            [series_ref[g * group + i, :blocks, :] for i in range(group)], axis=0
        )
        both = jnp.concatenate([split_three(block), split_three(block * block)], axis=0)
        sums = jnp.dot(both, ones, preferred_element_type=jnp.float32)
        for i in range(group):
            windows = []
            for kind in range(2):
                at = (kind * group + i) * blocks
                slot = i * 2 + kind
                sums_ref[slot, :blocks, :] = sums[at : at + blocks]
                inside = lambda first: sums_ref[slot, first : first + pos_rows, :LANES]
                total = lambda first: sums_ref[slot, first : first + pos_rows, LANES:]
                near, far = inside(whole), inside(whole + 1)
                if part:
                    near = pltpu.roll(near, LANES - part, 1)
                    far = pltpu.roll(far, LANES - part, 1)
                window = jnp.where(lane < LANES - part, near, far + total(whole)) - inside(0)
                for b in range(whole):
                    window = window + total(b)
                windows.append(window)
            energy = windows[1] - windows[0] * windows[0] / length
            scale_ref[g * group + i] = 1.0 / jnp.sqrt(energy + 1e-05)
        return carry

    lax.fori_loop(0, groups, scale_group, 0)

    def channel(c, slot, totals):
        reach = pad_rows - 8
        here = series_ref[c, :reach, :]
        after = series_ref[c, 1 : reach + 1, :]
        for u in range(PARTS):
            if u == 0:
                moved = here
            else:
                moved = jnp.where(
                    lane < LANES - STEP * u,
                    pltpu.roll(here, LANES - STEP * u, 1),
                    pltpu.roll(after, LANES - STEP * u, 1),
                )
            shifted_ref[slot, u, :reach, :] = moved
        frames = jnp.concatenate(
            [
                jnp.concatenate(
                    [
                        shifted_ref[slot, u, j : j + pos_rows, :].astype(jnp.bfloat16)
                        for j in range(width // LANES)
                    ],
                    axis=1,
                )
                for u in range(PARTS)
            ],
            axis=0,
        )
        product = lax.dot_general(
            frames, copies_ref[c], (((1,), (1,)), ((), ())), preferred_element_type=jnp.float32
        )
        scale = scale_ref[c]
        turned = {}
        for u in range(PARTS):
            piece = product[u * pos_rows : (u + 1) * pos_rows]
            for k in range(PARTS):
                turned[u, k] = piece if k == 0 else pltpu.roll(piece, STEP * k, 1)
        result = []
        for t in range(templ_here):
            values = turned[0, (-t) % PARTS]
            for u in range(1, PARTS):
                values = jnp.where(lane >= STEP * u, turned[u, (u - t) % PARTS], values)
            picks_ref[slot, t] = values * scale
            offset = offsets_ref[t, c]
            down, right = offset // LANES, offset % LANES
            wanted = jnp.where(lane < right, down + 1, down)
            picked = picks_ref[slot, t, :lag_rows, :]
            for d in range(1, (OFFMAX + LANES - 1) // LANES + 1):
                picked = jnp.where(wanted == d, picks_ref[slot, t, d : d + lag_rows, :], picked)
            weight = inverse_ref[t, pl.ds(c, 1), :] * available_ref[t, c].astype(jnp.float32)
            picked = pltpu.roll(picked * weight, (LANES - right) % LANES, 1)
            result.append(totals[t] + picked)
        return tuple(result)

    def channel_group(g, totals):
        for i in range(group):
            totals = channel(g * group + i, i, totals)
        return totals

    empty = tuple(jnp.zeros((lag_rows, LANES), jnp.float32) for _ in range(templ_here))
    totals = lax.fori_loop(0, groups, channel_group, empty)

    for t in range(templ_here):
        stacks_ref[station, t] = totals[t]
    stack_copies = [
        send(stacks_ref.at[station], send_stack.at[k], recv_stack.at[k], stack_peer(k))
        for k in range(1, stations)
    ]
    for copy in stack_copies:
        copy.wait_recv()
    share = lag_rows // stations
    for t in range(templ_here):
        full, mine = stacks_ref[0, t], stacks_ref[0, t, pl.ds(station * share, share), :]
        for s in range(1, stations):
            full = full + stacks_ref[s, t]
            mine = mine + stacks_ref[s, t, pl.ds(station * share, share), :]
        power = jnp.sum(jnp.sum(full * full, axis=1, keepdims=True), axis=0, keepdims=True)
        mine = mine / jnp.sqrt(power / (lag_rows * LANES) + 1e-05)
        for r in range(share):
            out_ref[t : t + 1, r * LANES : (r + 1) * LANES] = mine[r : r + 1]
    for copy in stack_copies:
        copy.wait_send()


def shards(records, templates, offsets, available):
    channels, _ = records.shape
    templ_here, _, length = templates.shape
    blocks, stations = lax.axis_size("tmpl"), lax.axis_size("sta")
    inner = largest_divisor(blocks, 4)
    outer = blocks // inner
    lag_rows = (blocks * LANES - OFFMAX - length + 1) // LANES
    reach_rows = (OFFMAX + LANES - 1) // LANES
    pos_rows = round_up(lag_rows + reach_rows, 16)
    width = round_up(length + STEP - 1, LANES)
    pad_rows = round_up(max(pos_rows + width // LANES, blocks) + 1, 8) + 8
    group = largest_divisor(channels, 4)
    slot_rows = round_up(channels, 8)
    sizes = (templ_here, channels, length, outer, inner, stations, lag_rows, pos_rows, pad_rows,
             width, group, slot_rows)
    macs = channels * templ_here * STEP * width * PARTS * pos_rows
    return pl.pallas_call(
        functools.partial(detect_kernel, sizes),
        out_shape=jax.ShapeDtypeStruct((templ_here, lag_rows // stations * LANES), jnp.float32),
        in_specs=[pl.BlockSpec(memory_space=pltpu.SMEM)] * 2
        + [pl.BlockSpec(memory_space=pltpu.VMEM)] * 2,
        out_specs=pl.BlockSpec(memory_space=pltpu.VMEM),
        scratch_shapes=[
            pltpu.VMEM((blocks * slot_rows, LANES), jnp.float32),
            pltpu.VMEM((channels, pad_rows, LANES), jnp.float32),
            pltpu.VMEM((templ_here, channels, width), jnp.float32),
            pltpu.VMEM((templ_here, channels, LANES), jnp.float32),
            pltpu.VMEM((2 * group, pad_rows, 2 * LANES), jnp.float32),
            pltpu.VMEM((channels, pos_rows, LANES), jnp.float32),
            pltpu.VMEM((group, PARTS, pad_rows, LANES), jnp.float32),
            pltpu.VMEM((channels, templ_here * STEP, width), jnp.bfloat16),
            pltpu.VMEM((group, templ_here, pos_rows, LANES), jnp.float32),
            pltpu.VMEM((stations, templ_here, lag_rows, LANES), jnp.float32),
        ]
        + [pltpu.SemaphoreType.DMA((inner,))] * 2
        + [pltpu.SemaphoreType.DMA((outer,))] * 2
        + [pltpu.SemaphoreType.DMA((stations,))] * 2,
        compiler_params=pltpu.CompilerParams(
            collective_id=0, has_side_effects=True, vmem_limit_bytes=40 * 1024 * 1024
        ),
        cost_estimate=pl.CostEstimate(
            flops=2 * macs, bytes_accessed=4 * (records.size + templates.size), transcendentals=0
        ),
    )(offsets, available, records, templates)


def solution(mesh):
    in_specs = (P("sta", "tmpl"), P("tmpl", "sta", None), P("tmpl", "sta"), P("tmpl", "sta"))
    out_specs = P("tmpl", "sta")
    return jax.shard_map(shards, mesh=mesh, in_specs=in_specs, out_specs=out_specs, check_vma=False)
```

time: 75.7 us -> 40.4 us (0.53)
  blocking collectives: 49.8 us -> 0 us
  Pallas kernels: 22.8 us -> 38.4 us
  other arithmetic: 0.82 us -> 0 us
    all_gather x1 -> x0, blocking collectives: 46.5 us -> none  [shards(): whole = lax.all_gather(records, 'tmpl', axis=1, tiled=True)]
    pallas_call x1, Pallas kernels: 22.8 us -> 38.4 us  [shards(): pl.pallas_call(functools.partial(detect_kernel, sizes), out_shape=jax.Sha...]
    psum x1 -> x0, blocking collectives: 3.36 us -> none  [shards(): full_stack = lax.psum(partial_stack, 'sta')]
    unnamed x9 -> x8, local copies, waits for them, and re-layouts: 1.89 us -> 1.83 us
where the time goes in v1:
time: 40.4 us; the launch traced here: 40.2 us
  Pallas kernels  38.4 us (95%)
  local copies, waits for them, and re-layouts  1.83 us (5%)
    pallas_call x1, Pallas kernels, shards(): pl.pallas_call(functools.partial(detect_kernel, sizes), out_shape=jax.Sha...  38.4 us
    unnamed x8, local copies, waits for them, and re-layouts  1.83 us

profile of v1, /device:TPU:0, one launch (start us, length us, event | category | flops | bytes accessed | tf_op | source)
XLA Modules:
  0.0 40.2 jit_solution(4772271685453219125)
XLA Ops:
  0.0 0.0 copy-start.2
  0.0 0.0 copy-start.1
  0.0 0.0 copy-start
  0.0 1.2 %copy.5.templates_ref = f32[4,76,600]{2,1,0:T(8,128)S(1)} copy(f32[4,76,600]{2,0,1:T(4,128)} %param.5) | data formatting | bytes 1459200 | tf_op args[1]
  1.2 0.0 copy-done.2
  1.2 0.0 copy-done.1
  1.2 0.0 copy-done
  1.3 38.4 %shard_map.46 = f32[4,512]{1,0:T(4,128)S(1)} custom-call(s32[4,76]{1,0:T(4,128)S(1)} %copy-done.1, s32[4,76]{1,0:T(4,128)S(1)} %copy-done.2, f32[76,128]{1,0:T(8,128)S(1)} %copy-done, f32[4,76,600]{2,1,0:T(8,128)S(1)} %copy.5.templates_ref), custom_call_target="tpu_custom_call" | custom-call | flops 796917760 | bytes 768512 | tf_op jit(solution)/shard_map/pallas_call | solution.py:262
  39.6 0.6 %copy.7 = f32[4,512]{1,0:T(4,128)} copy(f32[4,512]{1,0:T(4,128)S(1)} %shard_map.46) | data formatting | bytes 16384
Async XLA Ops:
  0.0 1.2 %copy-start.2 = (s32[4,76]{1,0:T(4,128)S(1)}, s32[4,76]{1,0:T(4,128)}, u32[]{:S(2)}) copy-start(s32[4,76]{1,0:T(4,128)} %available_ref.1) | copy-start | bytes 3652
  0.0 1.2 %copy-start.1 = (s32[4,76]{1,0:T(4,128)S(1)}, s32[4,76]{1,0:T(4,128)}, u32[]{:S(2)}) copy-start(s32[4,76]{1,0:T(4,128)} %offsets_ref.1) | copy-start | bytes 3652
  0.0 1.2 %copy-start = (f32[76,128]{1,0:T(8,128)S(1)}, f32[76,128]{1,0:T(8,128)}, u32[]{:S(2)}) copy-start(f32[76,128]{1,0:T(8,128)} %records_ref.1) | copy-start | bytes 116740

commit v2 on v1

v2 whole, which is shorter than its diff:
```python
import functools

import jax
import jax.numpy as jnp
from jax import lax
from jax.experimental import pallas as pl
from jax.experimental.pallas import tpu as pltpu
from jax.sharding import PartitionSpec as P

OFFMAX = 425
LANES = 128
STEP = 32
PARTS = LANES // STEP


def round_up(value, unit):
    return (value + unit - 1) // unit * unit


def largest_divisor(value, most):
    return max(d for d in range(1, most + 1) if value % d == 0)


def split_three(values):
    high = values.astype(jnp.bfloat16)
    rest = values - high.astype(jnp.float32)
    middle = rest.astype(jnp.bfloat16)
    low = (rest - middle.astype(jnp.float32)).astype(jnp.bfloat16)
    return jnp.concatenate([high, middle, low], axis=1)


def detect_kernel(
    sizes, offsets_ref, available_ref, records_ref, templates_hbm, out_ref,
    templates_ref, gathered_ref, series_ref, centred_ref, inverse_ref, sums_ref, shifted_ref,
    copies_ref, picks_ref, stacks_ref, load_sem, send_near, recv_near, send_far, recv_far,
    send_stack, recv_stack,
):
    (templ_here, channels, length, outer, inner, stations, lag_rows, pos_rows, pad_rows, width,
     group, chunk) = sizes
    blocks = outer * inner
    chunks = round_up(channels, chunk) // chunk
    whole, part = length // LANES, length % LANES
    lane = lax.broadcasted_iota(jnp.int32, (1, LANES), 1)
    place, station = lax.axis_index("tmpl"), lax.axis_index("sta")
    mine_out, mine_in = place // inner, place % inner

    def far_peer(k):
        return (lax.rem(mine_out + k, outer) * inner + mine_in, station)

    def near_peer(k):
        return (mine_out * inner + lax.rem(mine_in + k, inner), station)

    def stack_peer(k):
        return (place, lax.rem(station + k, stations))

    peers = [far_peer(k) for k in range(1, outer)]
    peers += [near_peer(k) for k in range(1, inner)]
    peers += [stack_peer(k) for k in range(1, stations)]
    barrier = pltpu.get_barrier_semaphore()
    for peer in peers:
        pl.semaphore_signal(barrier, inc=1, device_id=peer, device_id_type=pl.DeviceIdType.MESH)

    load = pltpu.make_async_copy(templates_hbm, templates_ref, load_sem.at[0])
    load.start()

    def own_rows(n):
        first = ((n * inner + mine_in) * outer + mine_out) * chunk
        return gathered_ref.at[pl.ds(pl.multiple_of(first, 8), chunk)]

    def line_rows(n):
        first = (n * inner + mine_in) * outer * chunk
        return gathered_ref.at[pl.ds(pl.multiple_of(first, 8), outer * chunk)]

    for n in range(chunks):
        rows = records_ref[n * chunk : min((n + 1) * chunk, channels), :]
        if rows.shape[0] < chunk:
            tail = jnp.zeros((chunk - rows.shape[0], LANES), jnp.float32)
            rows = jnp.concatenate([rows, tail], axis=0)
        own_rows(n)[...] = rows
    pl.semaphore_wait(barrier, len(peers))

    def copy_to(part_ref, send_sem, recv_sem, peer):
        return pltpu.make_async_remote_copy(
            src_ref=part_ref, dst_ref=part_ref, send_sem=send_sem, recv_sem=recv_sem,
            device_id=peer, device_id_type=pl.DeviceIdType.MESH,
        )

    def far_copies(n):
        return [
            copy_to(own_rows(n), send_far.at[k, n], recv_far.at[k, n], far_peer(k))
            for k in range(1, outer)
        ]

    def near_copies(n):
        return [
            copy_to(line_rows(n), send_near.at[k, n], recv_near.at[k, n], near_peer(k))
            for k in range(1, inner)
        ]

    for n in range(chunks):
        for copy in far_copies(n):
            copy.start()

    series_ref[...] = jnp.zeros_like(series_ref)
    sums_ref[...] = jnp.zeros_like(sums_ref)
    centred_ref[...] = jnp.zeros_like(centred_ref)
    load.wait()

    def delay_group(g, carry):
        for i in range(group):
            c = g * group + i
            shapes = templates_ref[c]
            centred = shapes - jnp.sum(shapes, axis=1, keepdims=True) / length
            power = jnp.sum(centred * centred, axis=1, keepdims=True)
            centred_ref[i, :templ_here, :length] = centred
            inverse_ref[c, :templ_here, :] = jnp.broadcast_to(
                1.0 / jnp.sqrt(power + 1e-05), (templ_here, LANES)
            )
            for t in range(templ_here):
                wave = jnp.broadcast_to(centred_ref[i, t : t + 1, :], (8, width))
                first = pltpu.roll(wave, 0, 1, stride=1, stride_axis=0)
                for h in range(STEP // 16):
                    pair = [
                        first if s == 0 else pltpu.roll(first, s, 1)
                        for s in (16 * h, 16 * h + 8)
                    ]
                    copies_ref[c, t * STEP + 16 * h : t * STEP + 16 * h + 16, :] = (
                        jnp.concatenate(pair, axis=0).astype(jnp.bfloat16)
                    )
        return carry

    groups = channels // group
    each = groups // (chunks + 1)

    def forward(n, carry):
        lax.fori_loop(n * each, n * each + each, delay_group, 0)
        for copy in far_copies(n):
            copy.wait_recv()
        for copy in near_copies(n):
            copy.start()
        return carry

    lax.fori_loop(0, chunks, forward, 0)
    lax.fori_loop(chunks * each, groups, delay_group, 0)

    row = lax.broadcasted_iota(jnp.int32, (LANES, 2 * LANES), 0)
    column = lax.broadcasted_iota(jnp.int32, (LANES, 2 * LANES), 1)
    ones = jnp.where((row < column) | (column >= LANES), 1.0, 0.0).astype(jnp.bfloat16)
    ones = jnp.concatenate([ones, ones, ones], axis=0)

    def block_sums(n, count):
        for i in range(count):
            c = n * chunk + i
            for o in range(outer):
                series_ref[c, o * inner : (o + 1) * inner, :] = gathered_ref[
                    pl.ds(n * blocks * chunk + o * chunk + i, inner, stride=outer * chunk), :
                ]
        block = jnp.concatenate(
            [series_ref[n * chunk + i, :blocks, :] for i in range(count)], axis=0
        )
        for kind in range(2):
            parts = split_three(block if kind == 0 else block * block)
            sums = jnp.dot(parts, ones, preferred_element_type=jnp.float32)
            for i in range(count):
                sums_ref[i, kind, :blocks, :] = sums[i * blocks : (i + 1) * blocks]

    def scale_of(i):
        windows = []
        for kind in range(2):
            inside = lambda first: sums_ref[i, kind, first : first + pos_rows, :LANES]
            total = lambda first: sums_ref[i, kind, first : first + pos_rows, LANES:]
            near, far = inside(whole), inside(whole + 1)
            if part:
                near = pltpu.roll(near, LANES - part, 1)
                far = pltpu.roll(far, LANES - part, 1)
            window = jnp.where(lane < LANES - part, near, far + total(whole)) - inside(0)
            for b in range(whole):
                window = window + total(b)
            windows.append(window)
        energy = windows[1] - windows[0] * windows[0] / length
        return 1.0 / jnp.sqrt(energy + 1e-05)

    def channel(c, inside_chunk, slot, totals):
        reach = pad_rows - 8
        for u in range(1, PARTS):
            shifted_ref[slot, u, :reach, :] = pltpu.roll(
                series_ref[c, :reach, :], LANES - STEP * u, 1
            )

        def frame(u, j):
            if u == 0:
                return series_ref[c, j : j + pos_rows, :].astype(jnp.bfloat16)
            return jnp.where(
                lane < LANES - STEP * u,
                shifted_ref[slot, u, j : j + pos_rows, :],
                shifted_ref[slot, u, j + 1 : j + 1 + pos_rows, :],
            ).astype(jnp.bfloat16)

        frames = jnp.concatenate(
            [
                jnp.concatenate(
                    [frame(u, j) for j in range(width // LANES)],
                    axis=1,
                )
                for u in range(PARTS)
            ],
            axis=0,
        )
        product = lax.dot_general(
            frames, copies_ref[c], (((1,), (1,)), ((), ())), preferred_element_type=jnp.float32
        )
        scale = scale_of(inside_chunk)
        turned = {}
        for u in range(PARTS):
            piece = product[u * pos_rows : (u + 1) * pos_rows]
            for k in range(PARTS):
                turned[u, k] = piece if k == 0 else pltpu.roll(piece, STEP * k, 1)
        result = []
        for t in range(templ_here):
            values = turned[0, (-t) % PARTS]
            for u in range(1, PARTS):
                values = jnp.where(lane >= STEP * u, turned[u, (u - t) % PARTS], values)
            picks_ref[slot, t] = values * scale
            offset = offsets_ref[t, c]
            down, right = offset // LANES, offset % LANES
            wanted = jnp.where(lane < right, down + 1, down)
            picked = picks_ref[slot, t, :lag_rows, :]
            for d in range(1, (OFFMAX + LANES - 1) // LANES + 1):
                picked = jnp.where(wanted == d, picks_ref[slot, t, d : d + lag_rows, :], picked)
            weight = inverse_ref[c, t : t + 1, :] * available_ref[t, c].astype(jnp.float32)
            picked = pltpu.roll(picked * weight, (LANES - right) % LANES, 1)
            result.append(totals[t] + picked)
        return tuple(result)

    def one_chunk(n, count, totals):
        for copy in near_copies(n):
            copy.wait_recv()
        block_sums(n, count)

        def channel_group(g, totals):
            for i in range(group):
                totals = channel(n * chunk + g * group + i, g * group + i, i, totals)
            return totals

        return lax.fori_loop(0, count // group, channel_group, totals)

    totals = tuple(jnp.zeros((lag_rows, LANES), jnp.float32) for _ in range(templ_here))
    full_chunks = channels // chunk
    totals = lax.fori_loop(0, full_chunks, lambda n, totals: one_chunk(n, chunk, totals), totals)
    if full_chunks < chunks:
        totals = one_chunk(full_chunks, channels - full_chunks * chunk, totals)

    for t in range(templ_here):
        stacks_ref[station, t] = totals[t]
    stack_copies = [
        copy_to(stacks_ref.at[station], send_stack.at[k], recv_stack.at[k], stack_peer(k))
        for k in range(1, stations)
    ]
    for copy in stack_copies:
        copy.start()
    for copy in stack_copies:
        copy.wait_recv()
    share = lag_rows // stations
    for t in range(templ_here):
        full, mine = stacks_ref[0, t], stacks_ref[0, t, pl.ds(station * share, share), :]
        for s in range(1, stations):
            full = full + stacks_ref[s, t]
            mine = mine + stacks_ref[s, t, pl.ds(station * share, share), :]
        power = jnp.sum(jnp.sum(full * full, axis=1, keepdims=True), axis=0, keepdims=True)
        mine = mine / jnp.sqrt(power / (lag_rows * LANES) + 1e-05)
        for r in range(share):
            out_ref[t : t + 1, r * LANES : (r + 1) * LANES] = mine[r : r + 1]
    for copy in stack_copies:
        copy.wait_send()
    for n in range(chunks):
        for copy in far_copies(n) + near_copies(n):
            copy.wait_send()


def shards(records, templates, offsets, available):
    channels, _ = records.shape
    templ_here, _, length = templates.shape
    blocks, stations = lax.axis_size("tmpl"), lax.axis_size("sta")
    inner = largest_divisor(blocks, 4)
    outer = blocks // inner
    lag_rows = (blocks * LANES - OFFMAX - length + 1) // LANES
    reach_rows = (OFFMAX + LANES - 1) // LANES
    pos_rows = round_up(lag_rows + reach_rows, 16)
    width = round_up(length + STEP - 1, LANES)
    pad_rows = round_up(max(pos_rows + width // LANES, blocks) + 1, 8) + 8
    group = largest_divisor(channels, 4)
    slot_rows = round_up(channels, 8)
    chunk = 16 if slot_rows % 16 == 0 else 8
    chunks = slot_rows // chunk
    sizes = (templ_here, channels, length, outer, inner, stations, lag_rows, pos_rows, pad_rows,
             width, group, chunk)
    macs = channels * templ_here * STEP * width * PARTS * pos_rows
    return pl.pallas_call(
        functools.partial(detect_kernel, sizes),
        out_shape=jax.ShapeDtypeStruct((templ_here, lag_rows // stations * LANES), jnp.float32),
        in_specs=[pl.BlockSpec(memory_space=pltpu.SMEM)] * 2
        + [pl.BlockSpec(memory_space=pltpu.VMEM), pl.BlockSpec(memory_space=pltpu.HBM)],
        out_specs=pl.BlockSpec(memory_space=pltpu.VMEM),
        scratch_shapes=[
            pltpu.VMEM((channels, templ_here, length), jnp.float32),
            pltpu.VMEM((blocks * slot_rows, LANES), jnp.float32),
            pltpu.VMEM((channels, pad_rows, LANES), jnp.float32),
            pltpu.VMEM((group, round_up(templ_here, 8), width), jnp.float32),
            pltpu.VMEM((channels, round_up(templ_here, 8), LANES), jnp.float32),
            pltpu.VMEM((chunk, 2, pad_rows, 2 * LANES), jnp.float32),
            pltpu.VMEM((group, PARTS, pad_rows, LANES), jnp.float32),
            pltpu.VMEM((channels, templ_here * STEP, width), jnp.bfloat16),
            pltpu.VMEM((group, templ_here, pos_rows, LANES), jnp.float32),
            pltpu.VMEM((stations, templ_here, lag_rows, LANES), jnp.float32),
        ]
        + [pltpu.SemaphoreType.DMA((1,))]
        + [pltpu.SemaphoreType.DMA((inner, chunks))] * 2
        + [pltpu.SemaphoreType.DMA((outer, chunks))] * 2
        + [pltpu.SemaphoreType.DMA((stations,))] * 2,
        compiler_params=pltpu.CompilerParams(
            collective_id=0, has_side_effects=True, vmem_limit_bytes=40 * 1024 * 1024
        ),
        cost_estimate=pl.CostEstimate(
            flops=2 * macs, bytes_accessed=4 * (records.size + templates.size), transcendentals=0
        ),
    )(offsets, available, records, jnp.transpose(templates, (1, 0, 2)))


def solution(mesh):
    in_specs = (P("sta", "tmpl"), P("tmpl", "sta", None), P("tmpl", "sta"), P("tmpl", "sta"))
    out_specs = P("tmpl", "sta")
    return jax.shard_map(shards, mesh=mesh, in_specs=in_specs, out_specs=out_specs, check_vma=False)
```

time: 40.4 us -> 39.7 us (0.983)
  Pallas kernels: 38.4 us -> 35.5 us
  local copies, waits for them, and re-layouts: 1.83 us -> 3.87 us
    pallas_call x1, Pallas kernels: 38.4 us -> 35.5 us  [shards(): pl.pallas_call(functools.partial(detect_kernel, sizes), out_shape=jax.Sha...]
    unnamed x8 -> x9, local copies, waits for them, and re-layouts: 1.83 us -> 3.87 us
where the time goes in v2:
time: 39.7 us; the launch traced here: 39.4 us
  Pallas kernels  35.5 us (89%)
  local copies, waits for them, and re-layouts  3.87 us (10%)
    pallas_call x1, Pallas kernels, shards(): pl.pallas_call(functools.partial(detect_kernel, sizes), out_shape=jax.Sha...  35.5 us
    unnamed x9, local copies, waits for them, and re-layouts  3.87 us

profile of v2, /device:TPU:0, one launch (start us, length us, event | category | flops | bytes accessed | tf_op | source)
XLA Modules:
  0.0 39.4 jit_solution(4767224846842210064)
XLA Ops:
  0.0 0.0 copy-start
  0.0 1.1 %copy-done = f32[4,76,600]{2,0,1:T(4,128)S(1)} copy-done((f32[4,76,600]{2,0,1:T(4,128)S(1)}, f32[4,76,600]{2,0,1:T(4,128)}, u32[]{:S(2)}) %copy-start) | copy-done | bytes 729624
  1.1 0.0 copy-start.1
  1.1 0.8 %copy-done.1 = f32[76,128]{1,0:T(8,128)S(1)} copy-done((f32[76,128]{1,0:T(8,128)S(1)}, f32[76,128]{1,0:T(8,128)}, u32[]{:S(2)}) %copy-start.1) | copy-done | bytes 38936
  1.9 0.0 copy-start.2
  1.9 0.7 %copy-done.2 = s32[4,76]{1,0:T(4,128)S(1)} copy-done((s32[4,76]{1,0:T(4,128)S(1)}, s32[4,76]{1,0:T(4,128)}, u32[]{:S(2)}) %copy-start.2) | copy-done | bytes 1240
  2.6 0.0 copy-start.3
  2.6 0.7 %copy-done.3 = s32[4,76]{1,0:T(4,128)S(1)} copy-done((s32[4,76]{1,0:T(4,128)S(1)}, s32[4,76]{1,0:T(4,128)}, u32[]{:S(2)}) %copy-start.3) | copy-done | bytes 1240
  3.3 35.5 %shard_map.46 = f32[4,512]{1,0:T(4,128)S(1)} custom-call(s32[4,76]{1,0:T(4,128)S(1)} %copy-done.2, s32[4,76]{1,0:T(4,128)S(1)} %copy-done.3, f32[76,128]{1,0:T(8,128)S(1)} %copy-done.1, f32[76,4,600]{2,1,0:T(4,128)S(1)} %bitcast.1), custom_call_target="tpu_custom_call" | custom-call | flops 796917760 | bytes 768512 | tf_op jit(solution)/shard_map/pallas_call | solution.py:298
  38.8 0.6 %copy.6 = f32[4,512]{1,0:T(4,128)} copy(f32[4,512]{1,0:T(4,128)S(1)} %shard_map.46) | data formatting | bytes 16384
Async XLA Ops:
  0.0 1.1 %copy-start = (f32[4,76,600]{2,0,1:T(4,128)S(1)}, f32[4,76,600]{2,0,1:T(4,128)}, u32[]{:S(2)}) copy-start(f32[4,76,600]{2,0,1:T(4,128)} %param.5) | copy-start | bytes 2188804
  1.1 0.8 %copy-start.1 = (f32[76,128]{1,0:T(8,128)S(1)}, f32[76,128]{1,0:T(8,128)}, u32[]{:S(2)}) copy-start(f32[76,128]{1,0:T(8,128)} %records_ref.1) | copy-start | bytes 116740
  1.9 0.7 %copy-start.2 = (s32[4,76]{1,0:T(4,128)S(1)}, s32[4,76]{1,0:T(4,128)}, u32[]{:S(2)}) copy-start(s32[4,76]{1,0:T(4,128)} %offsets_ref.1) | copy-start | bytes 3652
  2.6 0.7 %copy-start.3 = (s32[4,76]{1,0:T(4,128)S(1)}, s32[4,76]{1,0:T(4,128)}, u32[]{:S(2)}) copy-start(s32[4,76]{1,0:T(4,128)} %available_ref.1) | copy-start | bytes 3652

commit v3 on v2

--- a/solution.py
+++ b/solution.py
@@ -30,9 +30,10 @@
 
 
 def detect_kernel(
-    sizes, offsets_ref, available_ref, records_ref, templates_hbm, out_ref,
-    templates_ref, gathered_ref, series_ref, centred_ref, inverse_ref, sums_ref, shifted_ref,
-    copies_ref, picks_ref, stacks_ref, load_sem, send_near, recv_near, send_far, recv_far,
+    sizes, offsets_hbm, available_hbm, records_hbm, templates_hbm, out_ref,
+    offsets_ref, available_ref, records_ref, templates_ref, gathered_ref, series_ref, centred_ref,
+    inverse_ref, sums_ref, scale_ref, shifted_ref, frames_ref, copies_ref, products_ref, picks_ref,
+    stacks_ref, load_sem, send_near, recv_near, send_far, recv_far,
     send_stack, recv_stack,
 ):
     (templ_here, channels, length, outer, inner, stations, lag_rows, pos_rows, pad_rows, width,
@@ -60,8 +61,15 @@
     for peer in peers:
         pl.semaphore_signal(barrier, inc=1, device_id=peer, device_id_type=pl.DeviceIdType.MESH)
 
-    load = pltpu.make_async_copy(templates_hbm, templates_ref, load_sem.at[0])
-    load.start()
+    loads = [
+        pltpu.make_async_copy(source, target, load_sem.at[at])
+        for at, (source, target) in enumerate((
+            (records_hbm, records_ref), (templates_hbm, templates_ref),
+            (offsets_hbm, offsets_ref), (available_hbm, available_ref),
+        ))
+    ]
+    for load in loads:
+        load.start()
 
     def own_rows(n):
         first = ((n * inner + mine_in) * outer + mine_out) * chunk
@@ -71,6 +79,7 @@
         first = (n * inner + mine_in) * outer * chunk
         return gathered_ref.at[pl.ds(pl.multiple_of(first, 8), outer * chunk)]
 
+    loads[0].wait()
     for n in range(chunks):
         rows = records_ref[n * chunk : min((n + 1) * chunk, channels), :]
         if rows.shape[0] < chunk:
@@ -101,23 +110,28 @@
         for copy in far_copies(n):
             copy.start()
 
-    series_ref[...] = jnp.zeros_like(series_ref)
-    sums_ref[...] = jnp.zeros_like(sums_ref)
-    centred_ref[...] = jnp.zeros_like(centred_ref)
-    load.wait()
-
-    def delay_group(g, carry):
+    for ref in (series_ref, sums_ref, centred_ref, scale_ref, frames_ref, products_ref):
+        ref[...] = jnp.zeros_like(ref)
+    for load in loads[1:]:
+        load.wait()
+
+    def centre_group(g, carry):
         for i in range(group):
             c = g * group + i
             shapes = templates_ref[c]
             centred = shapes - jnp.sum(shapes, axis=1, keepdims=True) / length
             power = jnp.sum(centred * centred, axis=1, keepdims=True)
-            centred_ref[i, :templ_here, :length] = centred
+            centred_ref[c, :templ_here, :length] = centred
             inverse_ref[c, :templ_here, :] = jnp.broadcast_to(
                 1.0 / jnp.sqrt(power + 1e-05), (templ_here, LANES)
             )
+        return carry
+
+    def delay_group(g, carry):
+        for i in range(group):
+            c = g * group + i
             for t in range(templ_here):
-                wave = jnp.broadcast_to(centred_ref[i, t : t + 1, :], (8, width))
+                wave = jnp.broadcast_to(centred_ref[c, t : t + 1, :], (8, width))
                 first = pltpu.roll(wave, 0, 1, stride=1, stride_axis=0)
                 for h in range(STEP // 16):
                     pair = [
@@ -131,6 +145,7 @@
 
     groups = channels // group
     each = groups // (chunks + 1)
+    lax.fori_loop(0, groups, centre_group, 0)
 
     def forward(n, carry):
         lax.fori_loop(n * each, n * each + each, delay_group, 0)
@@ -180,39 +195,38 @@
         energy = windows[1] - windows[0] * windows[0] / length
         return 1.0 / jnp.sqrt(energy + 1e-05)
 
-    def channel(c, inside_chunk, slot, totals):
+    def frame_channel(c, inside_chunk, slot):
         reach = pad_rows - 8
         for u in range(1, PARTS):
             shifted_ref[slot, u, :reach, :] = pltpu.roll(
                 series_ref[c, :reach, :], LANES - STEP * u, 1
             )
-
-        def frame(u, j):
-            if u == 0:
-                return series_ref[c, j : j + pos_rows, :].astype(jnp.bfloat16)
-            return jnp.where(
-                lane < LANES - STEP * u,
-                shifted_ref[slot, u, j : j + pos_rows, :],
-                shifted_ref[slot, u, j + 1 : j + 1 + pos_rows, :],
-            ).astype(jnp.bfloat16)
-
-        frames = jnp.concatenate(
-            [
-                jnp.concatenate(
-                    [frame(u, j) for j in range(width // LANES)],
-                    axis=1,
-                )
-                for u in range(PARTS)
-            ],
-            axis=0,
+        for u in range(PARTS):
+            for j in range(width // LANES):
+                if u == 0:
+                    frame = series_ref[c, j : j + pos_rows, :]
+                else:
+                    frame = jnp.where(
+                        lane < LANES - STEP * u,
+                        shifted_ref[slot, u, j : j + pos_rows, :],
+                        shifted_ref[slot, u, j + 1 : j + 1 + pos_rows, :],
+                    )
+                frames_ref[
+                    slot, u * pos_rows : (u + 1) * pos_rows, j * LANES : (j + 1) * LANES
+                ] = frame.astype(jnp.bfloat16)
+        scale_ref[c] = scale_of(inside_chunk)
+
+    def multiply_channel(c, slot):
+        products_ref[slot] = lax.dot_general(
+            frames_ref[slot], copies_ref[c], (((1,), (1,)), ((), ())),
+            preferred_element_type=jnp.float32,
         )
-        product = lax.dot_general(
-            frames, copies_ref[c], (((1,), (1,)), ((), ())), preferred_element_type=jnp.float32
-        )
-        scale = scale_of(inside_chunk)
+
+    def pick_channel(c, slot, totals):
+        scale = scale_ref[c]
         turned = {}
         for u in range(PARTS):
-            piece = product[u * pos_rows : (u + 1) * pos_rows]
+            piece = products_ref[slot, u * pos_rows : (u + 1) * pos_rows, :]
             for k in range(PARTS):
                 turned[u, k] = piece if k == 0 else pltpu.roll(piece, STEP * k, 1)
         result = []
@@ -221,6 +235,7 @@
             for u in range(1, PARTS):
                 values = jnp.where(lane >= STEP * u, turned[u, (u - t) % PARTS], values)
             picks_ref[slot, t] = values * scale
+        for t in range(templ_here):
             offset = offsets_ref[t, c]
             down, right = offset // LANES, offset % LANES
             wanted = jnp.where(lane < right, down + 1, down)
@@ -232,14 +247,26 @@
             result.append(totals[t] + picked)
         return tuple(result)
 
+    def pick_group(g, totals):
+        for i in range(group):
+            totals = pick_channel(g * group + i, i, totals)
+        return totals
+
+    def multiply_group(g):
+        for i in range(group):
+            multiply_channel(g * group + i, i)
+
     def one_chunk(n, count, totals):
         for copy in near_copies(n):
             copy.wait_recv()
         block_sums(n, count)
 
-        def channel_group(g, totals):
+        def channel_group(h, totals):
+            g = n * (chunk // group) + h
+            totals = pick_group((g + groups - 2) % groups, totals)
+            multiply_group((g + groups - 1) % groups)
             for i in range(group):
-                totals = channel(n * chunk + g * group + i, g * group + i, i, totals)
+                frame_channel(g * group + i, h * group + i, i)
             return totals
 
         return lax.fori_loop(0, count // group, channel_group, totals)
@@ -249,6 +276,9 @@
     totals = lax.fori_loop(0, full_chunks, lambda n, totals: one_chunk(n, chunk, totals), totals)
     if full_chunks < chunks:
         totals = one_chunk(full_chunks, channels - full_chunks * chunk, totals)
+    totals = pick_group(groups - 2, totals)
+    multiply_group(groups - 1)
+    totals = pick_group(groups - 1, totals)
 
     for t in range(templ_here):
         stacks_ref[station, t] = totals[t]
@@ -298,27 +328,32 @@
     return pl.pallas_call(
         functools.partial(detect_kernel, sizes),
         out_shape=jax.ShapeDtypeStruct((templ_here, lag_rows // stations * LANES), jnp.float32),
-        in_specs=[pl.BlockSpec(memory_space=pltpu.SMEM)] * 2
-        + [pl.BlockSpec(memory_space=pltpu.VMEM), pl.BlockSpec(memory_space=pltpu.HBM)],
+        in_specs=[pl.BlockSpec(memory_space=pltpu.HBM)] * 4,
         out_specs=pl.BlockSpec(memory_space=pltpu.VMEM),
         scratch_shapes=[
+            pltpu.SMEM(offsets.shape, jnp.int32),
+            pltpu.SMEM(available.shape, jnp.int32),
+            pltpu.VMEM((channels, LANES), jnp.float32),
             pltpu.VMEM((channels, templ_here, length), jnp.float32),
             pltpu.VMEM((blocks * slot_rows, LANES), jnp.float32),
             pltpu.VMEM((channels, pad_rows, LANES), jnp.float32),
-            pltpu.VMEM((group, round_up(templ_here, 8), width), jnp.float32),
+            pltpu.VMEM((channels, round_up(templ_here, 8), width), jnp.float32),
             pltpu.VMEM((channels, round_up(templ_here, 8), LANES), jnp.float32),
             pltpu.VMEM((chunk, 2, pad_rows, 2 * LANES), jnp.float32),
+            pltpu.VMEM((channels, pos_rows, LANES), jnp.float32),
             pltpu.VMEM((group, PARTS, pad_rows, LANES), jnp.float32),
+            pltpu.VMEM((group, PARTS * pos_rows, width), jnp.bfloat16),
             pltpu.VMEM((channels, templ_here * STEP, width), jnp.bfloat16),
+            pltpu.VMEM((group, PARTS * pos_rows, templ_here * STEP), jnp.float32),
             pltpu.VMEM((group, templ_here, pos_rows, LANES), jnp.float32),
             pltpu.VMEM((stations, templ_here, lag_rows, LANES), jnp.float32),
         ]
-        + [pltpu.SemaphoreType.DMA((1,))]
+        + [pltpu.SemaphoreType.DMA((4,))]
         + [pltpu.SemaphoreType.DMA((inner, chunks))] * 2
         + [pltpu.SemaphoreType.DMA((outer, chunks))] * 2
         + [pltpu.SemaphoreType.DMA((stations,))] * 2,
         compiler_params=pltpu.CompilerParams(
-            collective_id=0, has_side_effects=True, vmem_limit_bytes=40 * 1024 * 1024
+            collective_id=0, has_side_effects=True, vmem_limit_bytes=60 * 1024 * 1024
         ),
         cost_estimate=pl.CostEstimate(
             flops=2 * macs, bytes_accessed=4 * (records.size + templates.size), transcendentals=0

time: 39.7 us -> 42.3 us (1.065)
  Pallas kernels: 35.5 us -> 40.8 us
  local copies, waits for them, and re-layouts: 3.87 us -> 1.3 us
    pallas_call x1, Pallas kernels: 35.5 us -> 40.8 us  [shards(): pl.pallas_call(functools.partial(detect_kernel, sizes), out_shape=jax.Sha...]
    unnamed x9 -> x1, local copies, waits for them, and re-layouts: 3.87 us -> 1.3 us
where the time goes in v3:
time: 42.3 us; the launch traced here: 42.1 us
  Pallas kernels  40.8 us (96%)
  local copies, waits for them, and re-layouts  1.3 us (3%)
    pallas_call x1, Pallas kernels, shards(): pl.pallas_call(functools.partial(detect_kernel, sizes), out_shape=jax.Sha...  40.8 us
    unnamed x1, local copies, waits for them, and re-layouts  1.3 us

profile of v3, /device:TPU:0, one launch (start us, length us, event | category | flops | bytes accessed | tf_op | source)
XLA Modules:
  0.0 42.1 jit_solution(6873557470720733448)
XLA Ops:
  0.0 40.8 %shard_map.46 = f32[4,512]{1,0:T(4,128)} custom-call(s32[4,76]{1,0:T(4,128)} %offsets_hbm.1, s32[4,76]{1,0:T(4,128)} %available_hbm.1, f32[76,128]{1,0:T(8,128)} %records_hbm.1, f32[76,4,600]{2,1,0:T(4,128)} %bitcast.1), custom_call_target="tpu_custom_call" | custom-call | flops 796917760 | bytes 768512 | tf_op jit(solution)/shard_map/pallas_call | solution.py:328
  40.8 1.3 %copy.6 = f32[4,512]{1,0:T(4,128)} copy(f32[4,512]{1,0:T(4,128)} %shard_map.46) | data formatting | bytes 16384

commit v4 on v2

v4 whole, which is shorter than its diff:
```python
import functools

import jax
import jax.numpy as jnp
from jax import lax
from jax.experimental import pallas as pl
from jax.experimental.pallas import tpu as pltpu
from jax.sharding import PartitionSpec as P

OFFMAX = 425
LANES = 128
STEP = 32
PARTS = LANES // STEP
CHUNK = 8


def round_up(value, unit):
    return (value + unit - 1) // unit * unit


def largest_divisor(value, most):
    return max(d for d in range(1, most + 1) if value % d == 0)


def split_three(values):
    high = values.astype(jnp.bfloat16)
    rest = values - high.astype(jnp.float32)
    middle = rest.astype(jnp.bfloat16)
    low = (rest - middle.astype(jnp.float32)).astype(jnp.bfloat16)
    return jnp.concatenate([high, middle, low], axis=1)


def detect_kernel(
    sizes, offsets_hbm, available_hbm, records_hbm, templates_hbm, out_ref,
    offsets_ref, available_ref, records_ref, templates_ref, gathered_ref, centred_ref, inverse_ref,
    scale_ref, moved_ref, copies_ref, picks_ref, stacks_ref, load_sem, send_near, recv_near, send_far, recv_far,
    send_stack, recv_stack,
):
    (templ_here, channels, length, outer, inner, stations, lag_rows, need_rows, pos_rows, rows,
     width) = sizes
    blocks = outer * inner
    chunk = CHUNK
    chunks = round_up(channels, chunk) // chunk
    whole, part = length // LANES, length % LANES
    lane = lax.broadcasted_iota(jnp.int32, (1, LANES), 1)
    place, station = lax.axis_index("tmpl"), lax.axis_index("sta")
    mine_out, mine_in = place // inner, place % inner

    def far_peer(k):
        return (lax.rem(mine_out + k, outer) * inner + mine_in, station)

    def near_peer(k):
        return (mine_out * inner + lax.rem(mine_in + k, inner), station)

    def stack_peer(k):
        return (place, lax.rem(station + k, stations))

    peers = [far_peer(k) for k in range(1, outer)]
    peers += [near_peer(k) for k in range(1, inner)]
    peers += [stack_peer(k) for k in range(1, stations)]
    barrier = pltpu.get_barrier_semaphore()
    for peer in peers:
        pl.semaphore_signal(barrier, inc=1, device_id=peer, device_id_type=pl.DeviceIdType.MESH)

    loads = [
        pltpu.make_async_copy(source, target, load_sem.at[at])
        for at, (source, target) in enumerate((
            (records_hbm, records_ref), (templates_hbm, templates_ref),
            (offsets_hbm, offsets_ref), (available_hbm, available_ref),
        ))
    ]
    for load in loads:
        load.start()

    def own_rows(n):
        first = ((n * inner + mine_in) * outer + mine_out) * chunk
        return gathered_ref.at[pl.ds(pl.multiple_of(first, 8), chunk)]

    def line_rows(n):
        first = (n * inner + mine_in) * outer * chunk
        return gathered_ref.at[pl.ds(pl.multiple_of(first, 8), outer * chunk)]

    loads[0].wait()
    for n in range(chunks):
        part_of = records_ref[n * chunk : min((n + 1) * chunk, channels), :]
        if part_of.shape[0] < chunk:
            tail = jnp.zeros((chunk - part_of.shape[0], LANES), jnp.float32)
            part_of = jnp.concatenate([part_of, tail], axis=0)
        own_rows(n)[...] = part_of
    pl.semaphore_wait(barrier, len(peers))

    def copy_to(part_ref, send_sem, recv_sem, peer):
        return pltpu.make_async_remote_copy(
            src_ref=part_ref, dst_ref=part_ref, send_sem=send_sem, recv_sem=recv_sem,
            device_id=peer, device_id_type=pl.DeviceIdType.MESH,
        )

    def far_copies(n):
        return [
            copy_to(own_rows(n), send_far.at[k, n], recv_far.at[k, n], far_peer(k))
            for k in range(1, outer)
        ]

    def near_copies(n):
        return [
            copy_to(line_rows(n), send_near.at[k, n], recv_near.at[k, n], near_peer(k))
            for k in range(1, inner)
        ]

    for n in range(chunks):
        for copy in far_copies(n):
            copy.start()

    for ref in (scale_ref, moved_ref):
        ref[...] = jnp.zeros_like(ref)
    filled = length // LANES * LANES
    centred_ref[:, :, filled:] = jnp.zeros(
        (channels, centred_ref.shape[1], width - filled), jnp.float32
    )
    for load in loads[1:]:
        load.wait()

    def centre_group(g, carry):
        for i in range(group):
            c = g * group + i
            shapes = templates_ref[c]
            centred = shapes - jnp.sum(shapes, axis=1, keepdims=True) / length
            power = jnp.sum(centred * centred, axis=1, keepdims=True)
            centred_ref[c, :templ_here, :length] = centred
            inverse_ref[c, :templ_here, :] = jnp.broadcast_to(
                1.0 / jnp.sqrt(power + 1e-05), (templ_here, LANES)
            )
        return carry

    def delay_channel(c):
        for t in range(templ_here):
            wave = jnp.broadcast_to(centred_ref[c, t : t + 1, :], (8, width))
            first = pltpu.roll(wave, 0, 1, stride=1, stride_axis=0)
            for h in range(STEP // 16):
                pair = [
                    first if s == 0 else pltpu.roll(first, s, 1) for s in (16 * h, 16 * h + 8)
                ]
                copies_ref[c, t * STEP + 16 * h : t * STEP + 16 * h + 16, :] = (
                    jnp.concatenate(pair, axis=0).astype(jnp.bfloat16)
                )

    group = largest_divisor(channels, 4)
    lax.fori_loop(0, channels // group, centre_group, 0)
    full_chunks = channels // chunk
    ahead = max(1, chunks // 2)
    each = chunks // ahead

    def forward(n):
        for copy in far_copies(n):
            copy.wait_recv()
        for copy in near_copies(n):
            copy.start()

    def early(n, carry):
        for i in range(chunk):
            delay_channel(n * chunk + i)
        for k in range(each):
            forward(n * each + k)
        return carry

    lax.fori_loop(0, ahead, early, 0)
    for n in range(ahead * each, chunks):
        forward(n)
    for c in range(full_chunks * chunk, channels):
        delay_channel(c)

    row = lax.broadcasted_iota(jnp.int32, (LANES, 2 * LANES), 0)
    column = lax.broadcasted_iota(jnp.int32, (LANES, 2 * LANES), 1)
    ones = jnp.where((row < column) | (column >= LANES), 1.0, 0.0).astype(jnp.bfloat16)
    ones = jnp.concatenate([ones, ones, ones], axis=0)

    def prepare(n):
        series = []
        for a in range(blocks):
            first = ((n * inner + a % inner) * outer + a // inner) * chunk
            series.append(gathered_ref[pl.ds(pl.multiple_of(first, 8), chunk), :])
        nothing = jnp.zeros((chunk, LANES), jnp.float32)
        at = lambda values, a: values[a] if a < blocks else nothing
        for u in range(PARTS):
            if u == 0:
                moved = series
            else:
                turned = [pltpu.roll(values, LANES - STEP * u, 1) for values in series]
                moved = [
                    jnp.where(lane < LANES - STEP * u, turned[a], at(turned, a + 1))
                    for a in range(blocks)
                ]
            for a in range(blocks):
                moved_ref[(u * rows + a) * chunk : (u * rows + a + 1) * chunk, :] = moved[a]
        block = jnp.concatenate(series, axis=0)
        both = jnp.concatenate([split_three(block), split_three(block * block)], axis=0)
        sums = jnp.dot(both, ones, preferred_element_type=jnp.float32)
        windows = []
        for kind in range(2):
            piece = [
                sums[(kind * blocks + a) * chunk : (kind * blocks + a + 1) * chunk]
                for a in range(blocks)
            ]
            inside = [values[:, :LANES] for values in piece]
            total = [values[:, LANES:] for values in piece]
            turned = [pltpu.roll(values, (LANES - part) % LANES, 1) for values in inside]
            window = []
            for a in range(need_rows):
                end = jnp.where(
                    lane < LANES - part,
                    at(turned, a + whole),
                    at(turned, a + whole + 1) + at(total, a + whole),
                )
                end = end - at(inside, a)
                for b in range(whole):
                    end = end + at(total, a + b)
                window.append(end)
            windows.append(window)
        for a in range(need_rows):
            energy = windows[1][a] - windows[0][a] * windows[0][a] / length
            scale_ref[a * chunk : (a + 1) * chunk, :] = lax.rsqrt(energy + 1e-05)

    def channel(n, i, totals):
        c = n * chunk + i
        frames = jnp.concatenate(
            [
                jnp.concatenate(
                    [
                        moved_ref[pl.ds((u * rows + j) * chunk + i, pos_rows, stride=chunk), :]
                        .astype(jnp.bfloat16)
                        for j in range(width // LANES)
                    ],
                    axis=1,
                )
                for u in range(PARTS)
            ],
            axis=0,
        )
        product = lax.dot_general(
            frames, copies_ref[c], (((1,), (1,)), ((), ())), preferred_element_type=jnp.float32
        )
        scale = scale_ref[pl.ds(i, pos_rows, stride=chunk), :]
        turned = {}
        for u in range(PARTS):
            piece = product[u * pos_rows : (u + 1) * pos_rows]
            for k in range(PARTS):
                turned[u, k] = piece if k == 0 else pltpu.roll(piece, STEP * k, 1)
        result = []
        for t in range(templ_here):
            values = turned[0, (-t) % PARTS]
            for u in range(1, PARTS):
                values = jnp.where(lane >= STEP * u, turned[u, (u - t) % PARTS], values)
            picks_ref[i, t] = values * scale
            offset = offsets_ref[t, c]
            down, right = offset // LANES, offset % LANES
            wanted = jnp.where(lane < right, down + 1, down)
            picked = picks_ref[i, t, :lag_rows, :]
            for d in range(1, (OFFMAX + LANES - 1) // LANES + 1):
                picked = jnp.where(wanted == d, picks_ref[i, t, d : d + lag_rows, :], picked)
            weight = inverse_ref[c, t : t + 1, :] * available_ref[t, c].astype(jnp.float32)
            picked = pltpu.roll(picked * weight, (LANES - right) % LANES, 1)
            result.append(totals[t] + picked)
        return tuple(result)

    def one_chunk(n, count, later, totals):
        for copy in near_copies(n):
            copy.wait_recv()
        prepare(n)
        for i in range(count):
            totals = channel(n, i, totals)
            if later:
                delay_channel((n + ahead) * chunk + i)
        return totals

    totals = tuple(jnp.zeros((lag_rows, LANES), jnp.float32) for _ in range(templ_here))
    split = full_chunks - ahead
    totals = lax.fori_loop(0, split, lambda n, now: one_chunk(n, chunk, True, now), totals)
    totals = lax.fori_loop(
        split, full_chunks, lambda n, now: one_chunk(n, chunk, False, now), totals
    )
    if full_chunks < chunks:
        totals = one_chunk(full_chunks, channels - full_chunks * chunk, False, totals)

    for t in range(templ_here):
        stacks_ref[station, t] = totals[t]
    stack_copies = [
        copy_to(stacks_ref.at[station], send_stack.at[k], recv_stack.at[k], stack_peer(k))
        for k in range(1, stations)
    ]
    for copy in stack_copies:
        copy.start()
    for copy in stack_copies:
        copy.wait_recv()
    share = lag_rows // stations
    for t in range(templ_here):
        full, mine = stacks_ref[0, t], stacks_ref[0, t, pl.ds(station * share, share), :]
        for s in range(1, stations):
            full = full + stacks_ref[s, t]
            mine = mine + stacks_ref[s, t, pl.ds(station * share, share), :]
        power = jnp.sum(jnp.sum(full * full, axis=1, keepdims=True), axis=0, keepdims=True)
        mine = mine / jnp.sqrt(power / (lag_rows * LANES) + 1e-05)
        for r in range(share):
            out_ref[t : t + 1, r * LANES : (r + 1) * LANES] = mine[r : r + 1]
    for copy in stack_copies:
        copy.wait_send()
    for n in range(chunks):
        for copy in far_copies(n) + near_copies(n):
            copy.wait_send()


def shards(records, templates, offsets, available):
    channels, _ = records.shape
    templ_here, _, length = templates.shape
    blocks, stations = lax.axis_size("tmpl"), lax.axis_size("sta")
    inner = largest_divisor(blocks, 4)
    outer = blocks // inner
    lag_rows = (blocks * LANES - OFFMAX - length + 1) // LANES
    need_rows = lag_rows + (OFFMAX + LANES - 1) // LANES
    pos_rows = round_up(need_rows, 16)
    width = round_up(length + STEP - 1, LANES)
    rows = max(pos_rows + width // LANES, blocks)
    chunks = round_up(channels, CHUNK) // CHUNK
    sizes = (templ_here, channels, length, outer, inner, stations, lag_rows, need_rows, pos_rows,
             rows, width)
    macs = channels * templ_here * STEP * width * PARTS * pos_rows
    return pl.pallas_call(
        functools.partial(detect_kernel, sizes),
        out_shape=jax.ShapeDtypeStruct((templ_here, lag_rows // stations * LANES), jnp.float32),
        in_specs=[pl.BlockSpec(memory_space=pltpu.HBM)] * 4,
        out_specs=pl.BlockSpec(memory_space=pltpu.VMEM),
        scratch_shapes=[
            pltpu.SMEM(offsets.shape, jnp.int32),
            pltpu.SMEM(available.shape, jnp.int32),
            pltpu.VMEM((channels, LANES), jnp.float32),
            pltpu.VMEM((channels, templ_here, length), jnp.float32),
            pltpu.VMEM((blocks * chunks * CHUNK, LANES), jnp.float32),
            pltpu.VMEM((channels, round_up(templ_here, 8), width), jnp.float32),
            pltpu.VMEM((channels, round_up(templ_here, 8), LANES), jnp.float32),
            pltpu.VMEM((pos_rows * CHUNK, LANES), jnp.float32),
            pltpu.VMEM((PARTS * rows * CHUNK, LANES), jnp.float32),
            pltpu.VMEM((channels, templ_here * STEP, width), jnp.bfloat16),
            pltpu.VMEM((CHUNK, templ_here, pos_rows, LANES), jnp.float32),
            pltpu.VMEM((stations, templ_here, lag_rows, LANES), jnp.float32),
        ]
        + [pltpu.SemaphoreType.DMA((4,))]
        + [pltpu.SemaphoreType.DMA((inner, chunks))] * 2
        + [pltpu.SemaphoreType.DMA((outer, chunks))] * 2
        + [pltpu.SemaphoreType.DMA((stations,))] * 2,
        compiler_params=pltpu.CompilerParams(
            collective_id=0, has_side_effects=True, vmem_limit_bytes=60 * 1024 * 1024
        ),
        cost_estimate=pl.CostEstimate(
            flops=2 * macs, bytes_accessed=4 * (records.size + templates.size), transcendentals=0
        ),
    )(offsets, available, records, jnp.transpose(templates, (1, 0, 2)))


def solution(mesh):
    in_specs = (P("sta", "tmpl"), P("tmpl", "sta", None), P("tmpl", "sta"), P("tmpl", "sta"))
    out_specs = P("tmpl", "sta")
    return jax.shard_map(shards, mesh=mesh, in_specs=in_specs, out_specs=out_specs, check_vma=False)
```

time: 39.7 us -> 41.9 us (1.055)
  Pallas kernels: 35.5 us -> 40.4 us
  local copies, waits for them, and re-layouts: 3.87 us -> 1.3 us
    pallas_call x1, Pallas kernels: 35.5 us -> 40.4 us  [shards(): pl.pallas_call(functools.partial(detect_kernel, sizes), out_shape=jax.Sha...]
    unnamed x9 -> x1, local copies, waits for them, and re-layouts: 3.87 us -> 1.3 us
where the time goes in v4:
time: 41.9 us; the launch traced here: 41.7 us
  Pallas kernels  40.4 us (96%)
  local copies, waits for them, and re-layouts  1.3 us (3%)
    pallas_call x1, Pallas kernels, shards(): pl.pallas_call(functools.partial(detect_kernel, sizes), out_shape=jax.Sha...  40.4 us
    unnamed x1, local copies, waits for them, and re-layouts  1.3 us

profile of v4, /device:TPU:0, one launch (start us, length us, event | category | flops | bytes accessed | tf_op | source)
XLA Modules:
  0.0 41.7 jit_solution(1149487171132945014)
XLA Ops:
  0.0 40.4 %shard_map.46 = f32[4,512]{1,0:T(4,128)} custom-call(s32[4,76]{1,0:T(4,128)} %offsets_hbm.1, s32[4,76]{1,0:T(4,128)} %available_hbm.1, f32[76,128]{1,0:T(8,128)} %records_hbm.1, f32[76,4,600]{2,1,0:T(4,128)} %bitcast.1), custom_call_target="tpu_custom_call" | custom-call | flops 796917760 | bytes 768512 | tf_op jit(solution)/shard_map/pallas_call | solution.py:326
  40.4 1.3 %copy.6 = f32[4,512]{1,0:T(4,128)} copy(f32[4,512]{1,0:T(4,128)} %shard_map.46) | data formatting | bytes 16384

commit v5 on v2

--- a/solution.py
+++ b/solution.py
@@ -30,8 +30,8 @@
 
 
 def detect_kernel(
-    sizes, offsets_ref, available_ref, records_ref, templates_hbm, out_ref,
-    templates_ref, gathered_ref, series_ref, centred_ref, inverse_ref, sums_ref, shifted_ref,
+    sizes, offsets_hbm, available_hbm, records_hbm, templates_hbm, out_ref,
+    offsets_ref, available_ref, records_ref, templates_ref, gathered_ref, series_ref, centred_ref, inverse_ref, sums_ref, shifted_ref,
     copies_ref, picks_ref, stacks_ref, load_sem, send_near, recv_near, send_far, recv_far,
     send_stack, recv_stack,
 ):
@@ -60,8 +60,15 @@
     for peer in peers:
         pl.semaphore_signal(barrier, inc=1, device_id=peer, device_id_type=pl.DeviceIdType.MESH)
 
-    load = pltpu.make_async_copy(templates_hbm, templates_ref, load_sem.at[0])
-    load.start()
+    loads = [
+        pltpu.make_async_copy(source, target, load_sem.at[at])
+        for at, (source, target) in enumerate((
+            (records_hbm, records_ref), (templates_hbm, templates_ref),
+            (offsets_hbm, offsets_ref), (available_hbm, available_ref),
+        ))
+    ]
+    for load in loads:
+        load.start()
 
     def own_rows(n):
         first = ((n * inner + mine_in) * outer + mine_out) * chunk
@@ -71,6 +78,7 @@
         first = (n * inner + mine_in) * outer * chunk
         return gathered_ref.at[pl.ds(pl.multiple_of(first, 8), outer * chunk)]
 
+    loads[0].wait()
     for n in range(chunks):
         rows = records_ref[n * chunk : min((n + 1) * chunk, channels), :]
         if rows.shape[0] < chunk:
@@ -104,7 +112,8 @@
     series_ref[...] = jnp.zeros_like(series_ref)
     sums_ref[...] = jnp.zeros_like(sums_ref)
     centred_ref[...] = jnp.zeros_like(centred_ref)
-    load.wait()
+    for load in loads[1:]:
+        load.wait()
 
     def delay_group(g, carry):
         for i in range(group):
@@ -130,7 +139,10 @@
         return carry
 
     groups = channels // group
-    each = groups // (chunks + 1)
+    full_chunks = channels // chunk
+    inline = full_chunks // 2
+    ahead = groups - inline * (chunk // group)
+    each = ahead // chunks
 
     def forward(n, carry):
         lax.fori_loop(n * each, n * each + each, delay_group, 0)
@@ -141,7 +153,7 @@
         return carry
 
     lax.fori_loop(0, chunks, forward, 0)
-    lax.fori_loop(chunks * each, groups, delay_group, 0)
+    lax.fori_loop(chunks * each, ahead, delay_group, 0)
 
     row = lax.broadcasted_iota(jnp.int32, (LANES, 2 * LANES), 0)
     column = lax.broadcasted_iota(jnp.int32, (LANES, 2 * LANES), 1)
@@ -178,7 +190,7 @@
                 window = window + total(b)
             windows.append(window)
         energy = windows[1] - windows[0] * windows[0] / length
-        return 1.0 / jnp.sqrt(energy + 1e-05)
+        return lax.rsqrt(energy + 1e-05)
 
     def channel(c, inside_chunk, slot, totals):
         reach = pad_rows - 8
@@ -232,7 +244,7 @@
             result.append(totals[t] + picked)
         return tuple(result)
 
-    def one_chunk(n, count, totals):
+    def one_chunk(n, count, later, totals):
         for copy in near_copies(n):
             copy.wait_recv()
         block_sums(n, count)
@@ -240,15 +252,19 @@
         def channel_group(g, totals):
             for i in range(group):
                 totals = channel(n * chunk + g * group + i, g * group + i, i, totals)
+            if later:
+                delay_group(ahead + n * (chunk // group) + g, 0)
             return totals
 
         return lax.fori_loop(0, count // group, channel_group, totals)
 
     totals = tuple(jnp.zeros((lag_rows, LANES), jnp.float32) for _ in range(templ_here))
-    full_chunks = channels // chunk
-    totals = lax.fori_loop(0, full_chunks, lambda n, totals: one_chunk(n, chunk, totals), totals)
+    totals = lax.fori_loop(0, inline, lambda n, now: one_chunk(n, chunk, True, now), totals)
+    totals = lax.fori_loop(
+        inline, full_chunks, lambda n, now: one_chunk(n, chunk, False, now), totals
+    )
     if full_chunks < chunks:
-        totals = one_chunk(full_chunks, channels - full_chunks * chunk, totals)
+        totals = one_chunk(full_chunks, channels - full_chunks * chunk, False, totals)
 
     for t in range(templ_here):
         stacks_ref[station, t] = totals[t]
@@ -298,10 +314,12 @@
     return pl.pallas_call(
         functools.partial(detect_kernel, sizes),
         out_shape=jax.ShapeDtypeStruct((templ_here, lag_rows // stations * LANES), jnp.float32),
-        in_specs=[pl.BlockSpec(memory_space=pltpu.SMEM)] * 2
-        + [pl.BlockSpec(memory_space=pltpu.VMEM), pl.BlockSpec(memory_space=pltpu.HBM)],
+        in_specs=[pl.BlockSpec(memory_space=pltpu.HBM)] * 4,
         out_specs=pl.BlockSpec(memory_space=pltpu.VMEM),
         scratch_shapes=[
+            pltpu.SMEM(offsets.shape, jnp.int32),
+            pltpu.SMEM(available.shape, jnp.int32),
+            pltpu.VMEM((channels, LANES), jnp.float32),
             pltpu.VMEM((channels, templ_here, length), jnp.float32),
             pltpu.VMEM((blocks * slot_rows, LANES), jnp.float32),
             pltpu.VMEM((channels, pad_rows, LANES), jnp.float32),
@@ -313,12 +331,12 @@
             pltpu.VMEM((group, templ_here, pos_rows, LANES), jnp.float32),
             pltpu.VMEM((stations, templ_here, lag_rows, LANES), jnp.float32),
         ]
-        + [pltpu.SemaphoreType.DMA((1,))]
+        + [pltpu.SemaphoreType.DMA((4,))]
         + [pltpu.SemaphoreType.DMA((inner, chunks))] * 2
         + [pltpu.SemaphoreType.DMA((outer, chunks))] * 2
         + [pltpu.SemaphoreType.DMA((stations,))] * 2,
         compiler_params=pltpu.CompilerParams(
-            collective_id=0, has_side_effects=True, vmem_limit_bytes=40 * 1024 * 1024
+            collective_id=0, has_side_effects=True, vmem_limit_bytes=60 * 1024 * 1024
         ),
         cost_estimate=pl.CostEstimate(
             flops=2 * macs, bytes_accessed=4 * (records.size + templates.size), transcendentals=0

time: 39.7 us -> 38.4 us (0.967)
  local copies, waits for them, and re-layouts: 3.87 us -> 1.3 us
  Pallas kernels: 35.5 us -> 36.9 us
    unnamed x9 -> x1, local copies, waits for them, and re-layouts: 3.87 us -> 1.3 us
    pallas_call x1, Pallas kernels: 35.5 us -> 36.9 us  [shards(): pl.pallas_call(functools.partial(detect_kernel, sizes), out_shape=jax.Sha...]
where the time goes in v5:
time: 38.4 us; the launch traced here: 38.2 us
  Pallas kernels  36.9 us (96%)
  local copies, waits for them, and re-layouts  1.3 us (3%)
    pallas_call x1, Pallas kernels, shards(): pl.pallas_call(functools.partial(detect_kernel, sizes), out_shape=jax.Sha...  36.9 us
    unnamed x1, local copies, waits for them, and re-layouts  1.3 us

profile of v5, /device:TPU:0, one launch (start us, length us, event | category | flops | bytes accessed | tf_op | source)
XLA Modules:
  0.0 38.2 jit_solution(10078978807114596028)
XLA Ops:
  0.0 36.9 %shard_map.46 = f32[4,512]{1,0:T(4,128)} custom-call(s32[4,76]{1,0:T(4,128)} %offsets_hbm.1, s32[4,76]{1,0:T(4,128)} %available_hbm.1, f32[76,128]{1,0:T(8,128)} %records_hbm.1, f32[76,4,600]{2,1,0:T(4,128)} %bitcast.1), custom_call_target="tpu_custom_call" | custom-call | flops 796917760 | bytes 768512 | tf_op jit(solution)/shard_map/pallas_call | solution.py:314
  36.9 1.3 %copy.6 = f32[4,512]{1,0:T(4,128)} copy(f32[4,512]{1,0:T(4,128)} %shard_map.46) | data formatting | bytes 16384
